TPU v7x, 256 devices: a whole 4x4x8 slice. The times are simulated.
256 devices in a mesh: rep: 32 (over x, y, core), node: 8 (over z).
Axes of the slice: x: 4, y: 4, z: 8, core: 2. Of those that a mesh axis runs over, the one named last changes fastest.
Arguments:
- attn_out: bfloat16 [32, 2560, 2048], P('rep', 'node'), may hold values from -0.125 to 0.125
- out_grad: bfloat16 [32, 2560, 3968], P('rep', 'node'), may hold values from -6 to 6
- weight: bfloat16 [2048, 3968], P('node'), may hold values from -0.09375 to 0.09375
- error: bfloat16 [32, 2048, 3968], P('rep', 'node'), may hold values from -6 to 6
- q_prev: float32 [8, 32, 3968], P('node'), may hold values from -6 to 6
Outputs:
- input_grad: bfloat16 [32, 2560, 2048], P('rep', 'node')
- new_error: bfloat16 [32, 2048, 3968], P('rep', 'node')
- p_out: float32 [32, 2048], P(None, 'node')
- q_out: float32 [8, 32, 3968], P('node')
All inputs are finite; a program needn't handle non-finite values.
Results may differ from a plain program's by a relative error of at most 0.00055.
Values may be sent and summed in bfloat16 or wider, within the bound.
A program may use at most 192 MiB of HBM per device.

v0:
```python
import jax
import jax.numpy as jnp
from jax import lax
from jax.sharding import PartitionSpec as P


def shards(attn_out, out_grad, weight, error, q_prev):
    highest = lax.Precision.HIGHEST
    feats = attn_out[0]
    cotan = out_grad[0]
    input_grad = lax.dot_general(
        cotan,
        lax.all_gather(weight, "node", axis=0, tiled=True),
        (((1,), (1,)), ((), ())),
        preferred_element_type=jnp.float32,
    ).astype(jnp.bfloat16)
    grad = lax.psum_scatter(
        lax.dot_general(feats, cotan, (((0,), (0,)), ((), ())), preferred_element_type=jnp.float32),
        "node",
        scatter_dimension=0,
        tiled=True,
    )
    memory = grad + error[0].astype(jnp.float32)
    left_local = lax.dot_general(
        q_prev[0],
        memory,
        (((1,), (1,)), ((), ())),
        precision=highest,
        preferred_element_type=jnp.float32,
    )
    left = lax.psum(left_local, "rep")
    gram = jnp.dot(left, left.T, precision=highest)
    lower_factor = jnp.linalg.cholesky(gram)
    basis = jax.scipy.linalg.solve_triangular(lower_factor, left, lower=True)
    right_local = jnp.dot(basis, memory, precision=highest)
    right = lax.psum(right_local, "rep") / lax.axis_size("rep")
    approx = lax.dot_general(
        basis,
        right,
        (((0,), (0,)), ((), ())),
        precision=highest,
        preferred_element_type=jnp.float32,
    )
    new_error = (memory - approx).astype(jnp.bfloat16)
    return (input_grad[None], new_error[None], basis, right[None])


def solution(mesh):
    in_specs = (
        P("rep", "node", None),
        P("rep", "node", None),
        P("node", None),
        P("rep", "node", None),
        P("node", None, None),
    )
    out_specs = (
        P("rep", "node", None),
        P("rep", "node", None),
        P(None, "node"),
        P("node", None, None),
    )
    return jax.shard_map(shards, mesh=mesh, in_specs=in_specs, out_specs=out_specs, check_vma=False)
```

profile of v0, /device:TPU:1, one launch (start us, length us, event | category | flops | bytes accessed | tf_op | source)
XLA Modules:
  0.0 648.6 jit_solution(1887771228479540567)
XLA Ops:
  7.2 0.0 copy-start
  7.2 0.0 reduce-scatter.2.cloned.1.call-start
  7.2 1.7 copy-done
  8.9 16.3 %fusion.2 = f32[2048,3968]{1,0:T(8,128)} fusion(bf16[1,320,3968]{2,1,0:T(8,128)(2,1)S(1)} %copy-done, bf16[1,320,2048]{2,1,0:T(8,128)(2,1)} %param.5), kind=kOutput, calls=%fused_computation.5 | convolution fusion | flops 5200936960 | bytes 36356096 | tf_op jit(solution)/shard_map/dot_general | solution.py:18
  25.2 0.0 copy-start.2
  25.2 0.0 reduce-scatter.2.cloned.1.call-update
  25.2 0.0 all-gather.2.cloned.1.call-start
  25.3 0.7 all-gather.2.cloned.1.call-update
  26.0 0.0 all-reduce.2.cloned.1.call-start
  26.0 324.2 %reduce-scatter.2.cloned.1.call-done = f32[256,3968]{1,0:T(8,128)} async-done(((f32[2048,3968]{1,0:T(8,128)}), f32[256,3968]{1,0:T(8,128)}) %reduce-scatter.2.cloned.1.call-update) | async-done | bytes 4063248 | tf_op jit(solution)/shard_map/reduce_scatter | solution.py:17
  350.2 0.0 copy-done.2
  350.2 6.3 fusion.11
  356.5 123.2 %psum.14 = f32[32,256]{1,0:T(8,128)S(1)} all-reduce(f32[32,256]{1,0:T(8,128)S(1)} %fusion.11), channel_id=1, replica_groups=mesh['rep'=32,'node'=8] {'rep'}, use_global_device_ids=true, to_apply=%region_1.0 | all-reduce | flops 8192 | bytes 65536 | tf_op jit(solution)/shard_map/psum | solution.py:31
  479.8 0.2 fusion.20
  479.9 0.1 copy.9
  480.0 2.9 cholesky.16
  483.0 0.6 compare_reduce_fusion
  483.6 0.7 fusion.15
  484.3 2.4 custom-call.7
  486.7 0.2 fusion.16
  487.0 0.0 copy-start.3
  487.0 6.1 fusion.8
  493.0 0.0 all-reduce.2.cloned.1.call-update
  493.1 25.4 %all-gather.2.cloned.1.call-done = bf16[2048,3968]{1,0:T(8,128)(2,1)} async-done(((bf16[256,3968]{1,0:T(8,128)(2,1)}), bf16[2048,3968]{1,0:T(8,128)(2,1)}) %all-gather.2.cloned.1.call-update) | async-done | bytes 16252944 | tf_op jit(solution)/shard_map/all_gather | solution.py:13
  518.5 10.4 %fusion.5 = bf16[1,320,2048]{2,1,0:T(8,128)(2,1)} fusion(bf16[2048,3968]{1,0:T(8,128)(2,1)} %all-gather.2.cloned.1.call-done, bf16[1,320,3968]{2,1,0:T(8,128)(2,1)S(1)} %copy-done), kind=kOutput, calls=%fused_computation.8 | convolution fusion | flops 5201592320 | bytes 20103168 | tf_op jit(solution)/shard_map/dot_general | solution.py:11
  528.9 105.6 %all-reduce.2.cloned.1.call-done = f32[32,3968]{1,0:T(8,128)} async-done(((f32[32,3968]{1,0:T(8,128)}), f32[32,3968]{1,0:T(8,128)}) %all-reduce.2.cloned.1.call-update) | async-done | bytes 507920 | tf_op jit(solution)/shard_map/psum | solution.py:36
  634.5 0.0 copy-done.3
  634.5 0.0 copy-start.1
  634.5 6.7 %fusion.1 = bf16[1,256,3968]{2,1,0:T(8,128)(2,1)} fusion(f32[32,256]{1,0:T(8,128)S(1)} %fusion.16, f32[256,3968]{1,0:T(8,128)} %reduce-scatter.2.cloned.1.call-done, bf16[1,256,3968]{2,1,0:T(8,128)(2,1)} %param.8, f32[32,3968]{1,0:T(8,128)} %all-reduce.2.cloned.1.call-done), kind=kOutput, calls=%fused_computation.2 | convolution fusion | flops 394260480 | bytes 8667136 | tf_op jit(solution)/shard_map/dot_general | solution.py:37
  641.3 0.0 copy-done.1
  641.3 0.8 multiply_bitcast_fusion
  (2 shorter events, 0.0 us)
Async XLA Ops:
  7.2 1.7 copy-start
  7.2 343.1 %reduce-scatter.2.cloned.1.call-start = ((), (), s32[]{:S(2)}) async-start(), calls=%async_computation.2 | async-start | bytes 36569088 | tf_op jit(solution)/shard_map/reduce_scatter | solution.py:17
  25.2 325.0 %copy-start.2 = (f32[1,32,3968]{2,1,0:T(8,128)S(1)}, f32[1,32,3968]{2,1,0:T(8,128)}, u32[]{:S(2)}) copy-start(f32[1,32,3968]{2,1,0:T(8,128)} %param.9) | copy-start | bytes 1523716
  25.2 493.3 %all-gather.2.cloned.1.call-start = ((), (), s32[]{:S(2)}) async-start(), calls=%async_computation.1 | async-start | bytes 18284544 | tf_op jit(solution)/shard_map/all_gather | solution.py:13
  26.0 608.5 %all-reduce.2.cloned.1.call-start = ((), (), s32[]{:S(2)}) async-start(), calls=%async_computation.3 | async-start | bytes 1015808 | tf_op jit(solution)/shard_map/psum | solution.py:36
  487.0 147.6 %copy-start.3 = (f32[32,256]{1,0:T(8,128)}, f32[32,256]{1,0:T(8,128)S(1)}, u32[]{:S(2)}) copy-start(f32[32,256]{1,0:T(8,128)S(1)} %fusion.16) | copy-start | bytes 98308
  634.5 6.7 %copy-start.1 = (f32[32,3968]{1,0:T(8,128)S(1)}, f32[32,3968]{1,0:T(8,128)}, u32[]{:S(2)}) copy-start(f32[32,3968]{1,0:T(8,128)} %all-reduce.2.cloned.1.call-done) | copy-start | bytes 1523716
Sparse Core Ops, SparseCore 0:
  25.4 324.8 reduce-scatter.1
  352.0 166.4 all-gather.1
  522.3 112.1 all-reduce.1
where the time goes:
time: 649 us
  waiting for transfers between devices  456 us (70%)
  blocking collectives  123 us (19%)
  matrix products  46.2 us (7%)
  between operations  13.8 us (2%)
  other arithmetic  7.51 us (1%)
    reduce_scatter x1, waiting for transfers between devices, shards(): lax.psum_scatter(lax.dot_general(feats, cotan, (((0,), (0,)), ((), ())),...  324 us
    psum x1, blocking collectives, shards(): left = lax.psum(left_local, 'rep')  123 us
    psum x1, waiting for transfers between devices, shards(): right = lax.psum(right_local, 'rep') / lax.axis_size('rep')  106 us
    all_gather x1, waiting for transfers between devices, shards(): lax.all_gather(weight, 'node', axis=0, tiled=True)  25.4 us
    dot_general x1, matrix products, shards(): lax.dot_general(feats, cotan, (((0,), (0,)), ((), ())), preferred_element...  16.3 us
  transfers between devices with their start and end apart: 3, of which 3 were waited for; matrix products, arithmetic and copies ran while one was open for 5% of the time, Pallas kernels for 0%

commit v1 on v0

--- a/solution.py
+++ b/solution.py
@@ -1,26 +1,168 @@
+import functools
+
 import jax
 import jax.numpy as jnp
 from jax import lax
+from jax.experimental import pallas as pl
+from jax.experimental.pallas import tpu as pltpu
 from jax.sharding import PartitionSpec as P
+
+MESH = pl.DeviceIdType.MESH
+NODES = 8
+TOK = 320
+SHARD = 256
+D = 3968
+WIDTHS = (512, 512, 512, 512, 512, 512, 512, 384)
+STARTS = tuple(sum(WIDTHS[:i]) for i in range(len(WIDTHS)))
+CHUNKS = len(WIDTHS)
+HALF = TOK // 2
+
+
+def gather_kernel(
+    a_ref, g_ref, err_ref, mem_ref,
+    gbuf, abuf, at, errbuf,
+    asend, arecv, gsend, grecv, lsem,
+):
+    me = lax.axis_index("node")
+
+    def peer(d):
+        return lax.rem(me + d + NODES, NODES)
+
+    barrier = pltpu.get_barrier_semaphore()
+    for d in range(1, NODES):
+        pl.semaphore_signal(barrier, inc=1, device_id={"node": peer(d)}, device_id_type=MESH)
+    own_g = pltpu.make_async_copy(g_ref, gbuf.at[me], lsem.at[0])
+    own_g.start()
+    own_a = pltpu.make_async_copy(
+        a_ref.at[:, pl.ds(pl.multiple_of(me * SHARD, SHARD), SHARD)], abuf.at[me], lsem.at[1]
+    )
+    own_a.start()
+    own_e = pltpu.make_async_copy(err_ref, errbuf, lsem.at[2])
+    own_e.start()
+    pl.semaphore_wait(barrier, NODES - 1)
+
+    def a_copy(d, slot):
+        to = peer(d)
+        return pltpu.make_async_remote_copy(
+            src_ref=a_ref.at[:, pl.ds(pl.multiple_of(to * SHARD, SHARD), SHARD)],
+            dst_ref=abuf.at[slot],
+            send_sem=asend.at[d],
+            recv_sem=arecv.at[d],
+            device_id={"node": to},
+            device_id_type=MESH,
+        )
+
+    def g_copy(way, chunk, hop, source):
+        rows = pl.ds(0, TOK) if hop < 3 else pl.ds(0 if way == 0 else HALF, HALF)
+        cols = pl.ds(STARTS[chunk], WIDTHS[chunk])
+        src = g_ref.at[:, cols] if hop == 0 else gbuf.at[source, rows, cols]
+        return pltpu.make_async_remote_copy(
+            src_ref=src,
+            dst_ref=gbuf.at[source, rows, cols],
+            send_sem=gsend.at[way, chunk, hop],
+            recv_sem=grecv.at[way, chunk, hop],
+            device_id={"node": peer(1 if way == 0 else -1)},
+            device_id_type=MESH,
+        )
+
+    def behind(way, n):
+        return peer(-n if way == 0 else n)
+
+    for d in (4, 3, 5, 2, 6, 1, 7):
+        a_copy(d, me).start()
+
+    def compute(chunk):
+        cols = pl.ds(STARTS[chunk], WIDTHS[chunk])
+        block = gbuf[:, :, cols].reshape(NODES * TOK, WIDTHS[chunk])
+        grad = jnp.dot(at[...], block, preferred_element_type=jnp.float32)
+        mem_ref[:, cols] = grad + errbuf[:, cols].astype(jnp.float32)
+
+    for t in range(CHUNKS + 4):
+        for hop in range(4):
+            chunk = t - hop
+            if 0 <= chunk < CHUNKS:
+                for way in range(2):
+                    if hop:
+                        g_copy(way, chunk, hop - 1, behind(way, hop)).wait_recv()
+                    g_copy(way, chunk, hop, behind(way, hop)).start()
+        if t == 3:
+            own_a.wait()
+            own_e.wait()
+            own_g.wait()
+            for d in range(1, NODES):
+                a_copy(d, peer(-d)).wait_recv()
+            at[...] = abuf[...].reshape(NODES * TOK, SHARD).T
+        if t >= 4:
+            chunk = t - 4
+            for way in range(2):
+                g_copy(way, chunk, 3, behind(way, 4)).wait_recv()
+            compute(chunk)
+    for d in range(1, NODES):
+        a_copy(d, me).wait_send()
+    for way in range(2):
+        for chunk in range(CHUNKS):
+            for hop in range(4):
+                g_copy(way, chunk, hop, behind(way, hop)).wait_send()
+
+
+def memory_of(a, g, err):
+    anywhere = pl.BlockSpec(memory_space=pl.ANY)
+    return pl.pallas_call(
+        gather_kernel,
+        out_shape=jax.ShapeDtypeStruct((SHARD, D), jnp.float32),
+        in_specs=[anywhere] * 3,
+        out_specs=pl.BlockSpec(memory_space=pltpu.VMEM),
+        scratch_shapes=[
+            pltpu.VMEM((NODES, TOK, D), jnp.bfloat16),
+            pltpu.VMEM((NODES, TOK, SHARD), jnp.bfloat16),
+            pltpu.VMEM((SHARD, NODES * TOK), jnp.bfloat16),
+            pltpu.VMEM((SHARD, D), jnp.bfloat16),
+            pltpu.SemaphoreType.DMA((NODES,)),
+            pltpu.SemaphoreType.DMA((NODES,)),
+            pltpu.SemaphoreType.DMA((2, CHUNKS, 4)),
+            pltpu.SemaphoreType.DMA((2, CHUNKS, 4)),
+            pltpu.SemaphoreType.DMA((3,)),
+        ],
+        compiler_params=pltpu.CompilerParams(
+            collective_id=0, has_side_effects=True, vmem_limit_bytes=48 * 2**20
+        ),
+        cost_estimate=pl.CostEstimate(flops=2 * 2560 * 256 * 3968 * 20, bytes_accessed=40 * 2**20, transcendentals=0),
+        name="gather_grad",
+    )(a, g, err)
+
+
+def back_kernel(g_ref, w_ref, out_ref):
+    w = w_ref[...].reshape(SHARD, D)
+    out_ref[...] = lax.dot_general(
+        g_ref[...], w, (((1,), (1,)), ((), ())), preferred_element_type=jnp.float32
+    ).astype(jnp.bfloat16)
+
+
+def back_of(g, w):
+    return pl.pallas_call(
+        back_kernel,
+        out_shape=jax.ShapeDtypeStruct((TOK, NODES * SHARD), jnp.bfloat16),
+        grid=(NODES,),
+        in_specs=[
+            pl.BlockSpec((TOK, D), lambda n: (0, 0)),
+            pl.BlockSpec((32, 1, 8, D), lambda n: (0, n, 0, 0)),
+        ],
+        out_specs=pl.BlockSpec((TOK, SHARD), lambda n: (0, n)),
+        compiler_params=pltpu.CompilerParams(vmem_limit_bytes=32 * 2**20),
+        name="input_grad",
+    )(g, w)
 
 
 def shards(attn_out, out_grad, weight, error, q_prev):
     highest = lax.Precision.HIGHEST
     feats = attn_out[0]
     cotan = out_grad[0]
-    input_grad = lax.dot_general(
-        cotan,
-        lax.all_gather(weight, "node", axis=0, tiled=True),
-        (((1,), (1,)), ((), ())),
-        preferred_element_type=jnp.float32,
-    ).astype(jnp.bfloat16)
-    grad = lax.psum_scatter(
-        lax.dot_general(feats, cotan, (((0,), (0,)), ((), ())), preferred_element_type=jnp.float32),
-        "node",
-        scatter_dimension=0,
-        tiled=True,
-    )
-    memory = grad + error[0].astype(jnp.float32)
+    at = lax.axis_index("rep")
+    piece = lax.dynamic_slice(weight, (at * 8, 0), (8, D))
+    column = lax.all_gather(piece, "node", axis=0)
+    whole = lax.all_gather(column, "rep", axis=0)
+    memory = memory_of(feats, cotan, error[0])
+    input_grad = back_of(cotan, whole)
     left_local = lax.dot_general(
         q_prev[0],
         memory,

time: 649 us -> 601 us (0.926)
  waiting for transfers between devices: 456 us -> 164 us
  Pallas kernels: 0 us -> 241 us
  matrix products: 46.2 us -> 17.8 us
  blocking collectives: 123 us -> 145 us
  local copies, waits for them, and re-layouts: 1.75 us -> 12.2 us
    reduce_scatter x1 -> x0, waiting for transfers between devices: 324 us -> none  [shards(): lax.psum_scatter(lax.dot_general(feats, cotan, (((0,), (0,)), ((), ())),...]
    pallas_call x0 -> x2, Pallas kernels: none -> 241 us  [the longest x1 232 us: memory_of(): pl.pallas_call(gather_kernel, out_shape=jax.ShapeDtypeStruct((SHARD, D),...]
    all_gather x1, waiting for transfers between devices: 25.4 us -> 71.9 us  [shards(): whole = lax.all_gather(column, 'rep', axis=0)]
    dot_general x2 -> x0, matrix products: 26.7 us -> none  [the longest x1 16.3 us: shards(): lax.dot_general(feats, cotan, (((0,), (0,)), ((), ())), preferred_element...]
    all_gather x0 -> x1, blocking collectives: none -> 21.4 us  [shards(): column = lax.all_gather(piece, 'node', axis=0)]
    psum x1, waiting for transfers between devices: 106 us -> 91.7 us  [shards(): right = lax.psum(right_local, 'rep') / lax.axis_size('rep')]
    unnamed x8 -> x18, local copies, waits for them, and re-layouts: 1.68 us -> 12.1 us
  transfers between devices with their start and end apart: 3 -> 2, of which waited for: 3 -> 2; matrix products, arithmetic and copies ran while one was open for 5% -> 1% of each run, Pallas kernels for 0% -> 0%
where the time goes in v1:
time: 601 us
  Pallas kernels  241 us (40%)
  waiting for transfers between devices  164 us (27%)
  blocking collectives  145 us (24%)
  matrix products  17.8 us (3%)
  between operations  14.1 us (2%)
  local copies, waits for them, and re-layouts  12.2 us (2%)
  other arithmetic  7.51 us (1%)
    pallas_call x1, Pallas kernels, memory_of(): pl.pallas_call(gather_kernel, out_shape=jax.ShapeDtypeStruct((SHARD, D),...  232 us
    psum x1, blocking collectives, shards(): left = lax.psum(left_local, 'rep')  123 us
    psum x1, waiting for transfers between devices, shards(): right = lax.psum(right_local, 'rep') / lax.axis_size('rep')  91.7 us
    all_gather x1, waiting for transfers between devices, shards(): whole = lax.all_gather(column, 'rep', axis=0)  71.9 us
    all_gather x1, blocking collectives, shards(): column = lax.all_gather(piece, 'node', axis=0)  21.4 us
    unnamed x18, local copies, waits for them, and re-layouts  12.1 us
  transfers between devices with their start and end apart: 2, of which 2 were waited for; matrix products, arithmetic and copies ran while one was open for 1% of the time, Pallas kernels for 0%

profile of v1, /device:TPU:1, one launch (start us, length us, event | category | flops | bytes accessed | tf_op | source)
XLA Modules:
  0.0 601.0 jit_solution(1086251375782096322)
XLA Ops:
  7.2 0.0 copy-start
  7.2 0.0 all-reduce.2.cloned.1.call-start
  7.2 0.0 copy-start.2
  7.2 1.8 copy-done.2
  9.1 0.0 copy-start.4
  9.1 1.6 copy-done.4
  10.7 0.0 copy-start.5
  10.7 1.3 copy-done.5
  12.0 0.0 copy-start.7
  12.0 231.9 %gather_grad.1 = f32[256,3968]{1,0:T(8,128)} custom-call(bf16[320,2048]{1,0:T(8,128)(2,1)S(1)} %bitcast.35, bf16[320,3968]{1,0:T(8,128)(2,1)S(1)} %bitcast.32, bf16[256,3968]{1,0:T(8,128)(2,1)S(1)} %bitcast.34), custom_call_target="tpu_custom_call" | custom-call | flops 104018739200 | bytes 41943040 | tf_op jit(solution)/shard_map/gather_grad/pallas_call | solution.py:110
  243.9 0.0 copy-done.7
  243.9 5.6 convolution_bitcast_fusion
  249.6 123.4 %psum.14 = f32[32,256]{1,0:T(8,128)S(1)} all-reduce(f32[32,256]{1,0:T(8,128)S(1)} %convolution_bitcast_fusion), channel_id=1, replica_groups=mesh['rep'=32,'node'=8] {'rep'}, use_global_device_ids=true, to_apply=%region_0.0 | all-reduce | flops 8192 | bytes 65536 | tf_op jit(solution)/shard_map/psum | solution.py:173
  373.0 0.2 fusion.10
  373.1 0.1 copy.10
  373.2 2.9 cholesky.16
  376.2 0.6 compare_reduce_fusion
  376.8 0.7 fusion.5
  377.5 2.4 custom-call.7
  379.9 0.2 fusion.6
  380.2 0.0 copy-start.8
  380.2 5.1 fusion.11
  385.3 0.0 all-reduce.2.cloned.1.call-update
  385.3 0.0 all-gather.4.cloned.1.call-start
  385.4 0.0 copy-done
  385.4 21.4 %all-gather = bf16[64,3968]{1,0:T(8,128)(2,1)} all-gather(bf16[8,3968]{1,0:T(8,128)(2,1)S(1)} %constant_dynamic-slice_fusion), channel_id=2, replica_groups=mesh['rep'=32,'node'=8] {'node'}, dimensions={0}, use_global_device_ids=true | all-gather | bytes 571392 | tf_op jit(solution)/shard_map/all_gather | solution.py:162
  406.8 0.0 all-gather.4.cloned.1.call-update
  406.8 91.7 %all-reduce.2.cloned.1.call-done = f32[32,3968]{1,0:T(8,128)} async-done(((f32[32,3968]{1,0:T(8,128)}), f32[32,3968]{1,0:T(8,128)}) %all-reduce.2.cloned.1.call-update) | async-done | bytes 507920 | tf_op jit(solution)/shard_map/psum | solution.py:178
  498.5 0.0 copy-start.6
  498.5 6.6 %fusion.1 = bf16[1,256,3968]{2,1,0:T(8,128)(2,1)} fusion(f32[256,3968]{1,0:T(8,128)} %gather_grad.1, f32[32,256]{1,0:T(8,128)S(1)} %fusion.6, f32[32,3968]{1,0:T(8,128)} %all-reduce.2.cloned.1.call-done), kind=kOutput, calls=%fused_computation.2 | convolution fusion | flops 392228864 | bytes 6635520 | tf_op jit(solution)/shard_map/dot_general | solution.py:179
  505.1 0.0 copy-done.8
  505.1 0.0 copy-done.6
  505.1 0.8 multiply_bitcast_fusion
  505.9 71.9 %all-gather.4.cloned.1.call-done = bf16[256,8,3968]{2,1,0:T(8,128)(2,1)} async-done(((bf16[8,8,3968]{2,1,0:T(8,128)(2,1)}), bf16[256,8,3968]{2,1,0:T(8,128)(2,1)}) %all-gather.4.cloned.1.call-update) | async-done | bytes 16252944 | tf_op jit(solution)/shard_map/all_gather | solution.py:163
  577.9 0.0 copy-start.1
  577.9 5.6 copy-done.1
  583.5 0.0 copy-start.3
  583.5 1.7 copy-done.3
  585.2 9.0 %input_grad.1 = bf16[320,2048]{1,0:T(8,128)(2,1)} custom-call(bf16[320,3968]{1,0:T(8,128)(2,1)S(1)} %bitcast.33, bf16[32,8,8,3968]{3,2,1,0:T(8,128)(2,1)S(1)} %bitcast.31), custom_call_target="tpu_custom_call" | custom-call | tf_op jit(solution)/shard_map/input_grad/pallas_call | solution.py:142
  (3 shorter events, 0.1 us)
Async XLA Ops:
  7.2 378.2 %copy-start = (bf16[256,3968]{1,0:T(8,128)(2,1)S(1)}, bf16[256,3968]{1,0:T(8,128)(2,1)}, u32[]{:S(2)}) copy-start(bf16[256,3968]{1,0:T(8,128)(2,1)} %param.7) | copy-start | bytes 6094852
  7.2 491.3 %all-reduce.2.cloned.1.call-start = ((), (), s32[]{:S(2)}) async-start(), calls=%async_computation | async-start | bytes 1015808 | tf_op jit(solution)/shard_map/psum | solution.py:178
  7.2 1.9 copy-start.2
  9.1 1.6 copy-start.4
  10.7 1.3 copy-start.5
  12.0 231.9 %copy-start.7 = (f32[1,32,3968]{2,1,0:T(8,128)S(1)}, f32[1,32,3968]{2,1,0:T(8,128)}, u32[]{:S(2)}) copy-start(f32[1,32,3968]{2,1,0:T(8,128)} %param.9) | copy-start | bytes 1523716
  380.2 125.0 %copy-start.8 = (f32[32,256]{1,0:T(8,128)}, f32[32,256]{1,0:T(8,128)S(1)}, u32[]{:S(2)}) copy-start(f32[32,256]{1,0:T(8,128)S(1)} %fusion.6) | copy-start | bytes 98308
  385.3 192.5 %all-gather.4.cloned.1.call-start = ((), (), s32[]{:S(2)}) async-start(), calls=%async_computation.1 | async-start | bytes 16760832 | tf_op jit(solution)/shard_map/all_gather | solution.py:163
  498.5 6.7 %copy-start.6 = (f32[32,3968]{1,0:T(8,128)S(1)}, f32[32,3968]{1,0:T(8,128)}, u32[]{:S(2)}) copy-start(f32[32,3968]{1,0:T(8,128)} %all-reduce.2.cloned.1.call-done) | copy-start | bytes 1523716
  577.9 5.6 copy-start.1
  583.5 1.7 copy-start.3
Sparse Core Ops, SparseCore 0:
  385.5 112.9 all-reduce.1
  501.4 76.4 all-gather.3

commit v2 on v0

v2 whole, which is shorter than its diff:
```python
import types

import jax
import jax.numpy as jnp
from jax import lax
from jax.experimental import pallas as pl
from jax.experimental.pallas import tpu as pltpu
from jax.sharding import PartitionSpec as P

MESH = pl.DeviceIdType.MESH
BF16, F32 = jnp.bfloat16, jnp.float32
NODES = 8
SIDE = 4
REPS = 32
TOK = 320
SHARD = 256
RANK = 32
FEATS = NODES * SHARD
D = 3968
WIDE = 4096
WIDTHS = (640, 640, 640, 640, 512, 512, 256, 128)
STARTS = tuple(sum(WIDTHS[:i]) for i in range(len(WIDTHS)))
CHUNKS = len(WIDTHS)
SPLIT = 160

DMA = pltpu.SemaphoreType.DMA
SCRATCH = dict(
    gbuf=pltpu.VMEM((NODES, TOK, D), BF16),
    abuf=pltpu.VMEM((NODES, TOK, SHARD), BF16),
    at=pltpu.VMEM((SHARD, NODES * TOK), BF16),
    avm=pltpu.VMEM((TOK, FEATS), BF16),
    errbuf=pltpu.VMEM((SHARD, D), BF16),
    mem=pltpu.VMEM((SHARD, D), F32),
    wbuf=pltpu.VMEM((NODES, SIDE, SIDE, 16, D), BF16),
    qbuf=pltpu.VMEM((NODES, RANK, WIDE), F32),
    qloc=pltpu.VMEM((RANK, WIDE), F32),
    qsp=pltpu.VMEM((3 * 2 * RANK, D), BF16),
    lbuf=pltpu.VMEM((NODES, RANK, SHARD), F32),
    lrx=pltpu.VMEM((NODES, RANK // 2, SHARD), F32),
    l2=pltpu.VMEM((NODES, RANK // 2, SHARD), F32),
    lz=pltpu.VMEM((NODES, RANK // 2, SHARD), F32),
    lx=pltpu.VMEM((SIDE, RANK // 2, SHARD), F32),
    ly=pltpu.VMEM((SIDE, RANK // 2, SHARD), F32),
    left=pltpu.VMEM((RANK, SHARD), F32),
    basis=pltpu.VMEM((RANK, SHARD), F32),
    b3=pltpu.VMEM((3 * RANK, SHARD), BF16),
    bt6=pltpu.VMEM((SHARD, 6 * RANK), BF16),
    rs=pltpu.VMEM((RANK, D), F32),
    rc=pltpu.VMEM((RANK, D), F32),
    rx=pltpu.VMEM((SIDE, RANK, D), F32),
    ry=pltpu.VMEM((SIDE, RANK, D), F32),
    qo=pltpu.VMEM((RANK, D), F32),
    local=DMA((8,)),
    out=DMA((CHUNKS,)),
    a_s=DMA((NODES,)), a_r=DMA((NODES,)),
    g_s=DMA((2, CHUNKS, 4)), g_r=DMA((2, CHUNKS, 4)),
    qz_s=DMA((4,)), qz_r=DMA((4,)),
    qx_s=DMA((4,)), qx_r=DMA((4,)),
    qy_s=DMA((4,)), qy_r=DMA((4,)),
    qc_s=DMA((1,)), qc_r=DMA((1,)),
    wz_s=DMA((4,)), wz_r=DMA((4,)),
    wx_s=DMA((2, 4)), wx_r=DMA((2, 4)),
    wy_s=DMA((2, 4)), wy_r=DMA((2, 4)),
    wc_s=DMA((4,)), wc_r=DMA((4,)),
    lc_s=DMA((2,)), lc_r=DMA((2,)),
    lz_s=DMA((NODES,)), lz_r=DMA((NODES,)),
    lx_s=DMA((4,)), lx_r=DMA((4,)),
    ly_s=DMA((4,)), ly_r=DMA((4,)),
    rc_s=DMA((CHUNKS,)), rc_r=DMA((CHUNKS,)),
    rx_s=DMA((CHUNKS, 4)), rx_r=DMA((CHUNKS, 4)),
    ry_s=DMA((CHUNKS, 4)), ry_r=DMA((CHUNKS, 4)),
)


def split3(value):
    high = value.astype(BF16)
    rest = value - high.astype(F32)
    middle = rest.astype(BF16)
    low = (rest - middle.astype(F32)).astype(BF16)
    return high, middle, low


def dot_nt(a, b):
    return lax.dot_general(a, b, (((1,), (1,)), ((), ())), preferred_element_type=F32)


def dot_nn(a, b):
    return jnp.dot(a, b, preferred_element_type=F32)


def thirds(value, rows):
    return value[:rows] + value[rows : 2 * rows] + value[2 * rows :]


def fused_kernel(
    a_hbm, g_hbm, w_hbm, e_hbm, q_hbm, ig_hbm, ne_hbm, p_hbm, qo_hbm, *scratch
):
    s = types.SimpleNamespace(**dict(zip(SCRATCH, scratch)))
    me = lax.axis_index("node")
    rep = lax.axis_index("rep")
    x = lax.div(rep, 2 * SIDE)
    y = lax.rem(lax.div(rep, 2), SIDE)
    core = lax.rem(rep, 2)
    chip = y * SIDE + x

    def node(d):
        return lax.rem(me + d + 2 * NODES, NODES)

    def along(v, k):
        return lax.rem(v + k + SIDE, SIDE)

    def z_peer(d):
        return {"node": node(d)}

    def x_peer(k):
        return {"rep": along(x, k) * 2 * SIDE + y * 2 + core}

    def y_peer(k):
        return {"rep": x * 2 * SIDE + along(y, k) * 2 + core}

    twin = {"rep": x * 2 * SIDE + y * 2 + (1 - core)}

    def remote(src, dst, send_sem, recv_sem, device):
        return pltpu.make_async_remote_copy(
            src_ref=src, dst_ref=dst, send_sem=send_sem, recv_sem=recv_sem,
            device_id=device, device_id_type=MESH,
        )

    def plane_of(slot):
        return lax.rem(me + jnp.where(slot < 4, 7 - slot, slot - 4), NODES)

    def part(start, size):
        return pl.ds(pl.multiple_of(start, size), size)

    mine = part(core * 4, 4)
    chip_cols = part(chip * 256, 256)

    barrier = pltpu.get_barrier_semaphore()
    friends = [z_peer(d) for d in range(1, NODES)]
    friends += [x_peer(k) for k in range(1, SIDE)] + [y_peer(k) for k in range(1, SIDE)] + [twin]
    for friend in friends:
        pl.semaphore_signal(barrier, inc=1, device_id=friend, device_id_type=MESH)

    own_q = pltpu.make_async_copy(q_hbm, s.qloc.at[:, pl.ds(0, D)], s.local.at[0])
    own_q.start()
    own_g = pltpu.make_async_copy(g_hbm, s.gbuf.at[me], s.local.at[1])
    own_g.start()
    own_a = pltpu.make_async_copy(a_hbm.at[:, part(me * SHARD, SHARD)], s.abuf.at[me], s.local.at[2])
    own_a.start()
    all_a = pltpu.make_async_copy(a_hbm, s.avm, s.local.at[3])
    all_a.start()
    own_e = pltpu.make_async_copy(e_hbm, s.errbuf, s.local.at[4])
    own_e.start()
    s.qloc[:, D:] = jnp.zeros((RANK, WIDE - D), F32)
    pl.semaphore_wait(barrier, len(friends))
    own_q.wait()

    def qz(i):
        slot = core * 4 + i
        d = jnp.where(core == 0, i + 1, -i)
        return remote(
            s.qloc.at[:, chip_cols], s.qbuf.at[slot, :, chip_cols], s.qz_s.at[i], s.qz_r.at[i], z_peer(d)
        )

    qz_own = pltpu.make_async_copy(s.qloc.at[:, chip_cols], s.qbuf.at[4, :, chip_cols], s.local.at[5])

    def only(which, action):
        pl.when(core == which)(action)

    def qz_start():
        only(0, lambda: qz(0).start())
        only(1, lambda: qz_own.start())
        for i in range(1, 4):
            qz(i).start()

    def qz_wait():
        only(0, lambda: qz(0).wait_recv())
        only(1, lambda: qz_own.wait())
        for i in range(1, 4):
            qz(i).wait_recv()

    def qz_sent():
        only(0, lambda: qz(0).wait_send())
        for i in range(1, 4):
            qz(i).wait_send()

    def qx(k, at):
        region = s.qbuf.at[mine, :, part((y * SIDE + at) * 256, 256)]
        return remote(region, region, s.qx_s.at[k], s.qx_r.at[k], x_peer(k))

    def qy(k, at):
        region = s.qbuf.at[mine, :, part(at * 1024, 1024)]
        return remote(region, region, s.qy_s.at[k], s.qy_r.at[k], y_peer(k))

    def qc(at):
        region = s.qbuf.at[part(at * 4, 4)]
        return remote(region, region, s.qc_s.at[0], s.qc_r.at[0], twin)

    w_rows = w_hbm.at[part(chip * 16, 16)]
    onward = {"node": lax.rem(me + jnp.where(core == 0, 1, NODES - 1), NODES)}

    def wz(i):
        slot = core * 4 + i
        src = w_rows if i == 0 else s.wbuf.at[slot - 1, y, x]
        return remote(src, s.wbuf.at[slot, y, x], s.wz_s.at[i], s.wz_r.at[i], onward)

    wz_own = pltpu.make_async_copy(w_rows, s.wbuf.at[4, y, x], s.local.at[6])

    def wz_start(i):
        if i == 0:
            only(0, lambda: wz(0).start())
            only(1, lambda: wz_own.start())
        else:
            wz(i).start()

    def wz_wait(i):
        if i == 0:
            only(0, lambda: wz(0).wait_recv())
            only(1, lambda: wz_own.wait())
        else:
            wz(i).wait_recv()

    def w_step(half, step, k, at):
        slots = part(core * 4 + 2 * half, 2)
        if (half == 0) == (step == 0):
            if step == 0:
                region = s.wbuf.at[slots, y, at]
            else:
                region = s.wbuf.at[slots, :, at]
            return remote(region, region, s.wx_s.at[half, k], s.wx_r.at[half, k], x_peer(k))
        if step == 0:
            region = s.wbuf.at[slots, at, x]
        else:
            region = s.wbuf.at[slots, at]
        return remote(region, region, s.wy_s.at[half, k], s.wy_r.at[half, k], y_peer(k))

    def w_where(half, step):
        return x if (half == 0) == (step == 0) else y

    def w_start(step):
        for half in range(2):
            for k in range(1, SIDE):
                w_step(half, step, k, w_where(half, step)).start()

    def w_wait(step):
        for half in range(2):
            for k in range(1, SIDE):
                w_step(half, step, k, along(w_where(half, step), -k)).wait_recv()

    def wc(i, at):
        region = s.wbuf.at[at * 4 + i]
        return remote(region, region, s.wc_s.at[i], s.wc_r.at[i], twin)

    def a_copy(d, at):
        to = node(d)
        return remote(a_hbm.at[:, part(to * SHARD, SHARD)], s.abuf.at[at], s.a_s.at[d], s.a_r.at[d], {"node": to})

    def g_copy(way, chunk, hop):
        source = node(-hop if way == 0 else hop)
        if hop < 3:
            rows = pl.ds(0, TOK)
        else:
            rows = pl.ds(0, SPLIT) if way == 0 else pl.ds(SPLIT, TOK - SPLIT)
        cols = pl.ds(STARTS[chunk], WIDTHS[chunk])
        dst = s.gbuf.at[source, rows, cols]
        src = g_hbm.at[:, cols] if hop == 0 else dst
        return remote(
            src, dst, s.g_s.at[way, chunk, hop], s.g_r.at[way, chunk, hop], z_peer(1 if way == 0 else -1)
        )

    def g_arrived(way, chunk, hop):
        source = node(-hop - 1 if way == 0 else hop + 1)
        if hop < 3:
            rows = pl.ds(0, TOK)
        else:
            rows = pl.ds(0, SPLIT) if way == 0 else pl.ds(SPLIT, TOK - SPLIT)
        region = s.gbuf.at[source, rows, pl.ds(STARTS[chunk], WIDTHS[chunk])]
        remote(
            region, region, s.g_s.at[way, chunk, hop], s.g_r.at[way, chunk, hop], z_peer(1 if way == 0 else -1)
        ).wait_recv()

    def left_terms():
        own_g.wait()
        all_a.wait()
        own_e.wait()

        def pair(half, carry):
            for i in range(2):
                pieces = split3(s.qbuf[2 * half + i, :, pl.ds(0, D)])
                for j in range(3):
                    s.qsp[pl.ds(64 * j + 32 * i, RANK), :] = pieces[j]
            pieces = split3(thirds(dot_nt(s.qsp[...], s.gbuf[me]), 2 * RANK))
            for i in range(2):
                plane = plane_of(2 * half + i)
                stacked = jnp.concatenate([piece[RANK * i : RANK * (i + 1)] for piece in pieces], axis=0)
                s.lbuf[plane] = thirds(dot_nn(stacked, s.avm[:, part(plane * SHARD, SHARD)]), RANK)
            return carry

        lax.fori_loop(0, 4, pair, 0)
        pieces = split3(s.qloc[:, pl.ds(0, D)])
        s.lbuf[me] += thirds(dot_nt(jnp.concatenate(pieces, axis=0), s.errbuf[...]), RANK)

    def lc0(at):
        return remote(
            s.lbuf.at[:, part((1 - at) * 16, 16)], s.lrx, s.lc_s.at[0], s.lc_r.at[0], twin
        )

    def lzc(d, at):
        to = node(d)
        return remote(s.l2.at[to], s.lz.at[at], s.lz_s.at[d], s.lz_r.at[d], {"node": to})

    def lxc(k, at):
        return remote(s.lx.at[at], s.lx.at[at], s.lx_s.at[k], s.lx_r.at[k], x_peer(k))

    def lyc(k, at):
        return remote(s.ly.at[at], s.ly.at[at], s.ly_s.at[k], s.ly_r.at[k], y_peer(k))

    def lc1(at):
        region = s.left.at[part(at * 16, 16)]
        return remote(region, region, s.lc_s.at[1], s.lc_r.at[1], twin)

    def left_0():
        left_terms()
        lc0(core).start()

    def left_1():
        lc0(core).wait_recv()
        s.l2[...] = s.lbuf[:, part(core * 16, 16), :] + s.lrx[...]
        for d in range(1, NODES):
            lzc(d, me).start()
        s.lz[me] = s.l2[me]

    def added(ref, count):
        total = ref[0]
        for i in range(1, count):
            total = total + ref[i]
        return total

    def left_2():
        for d in range(1, NODES):
            lzc(d, node(-d)).wait_recv()
        s.lx[x] = added(s.lz, NODES)
        for k in range(1, SIDE):
            lxc(k, x).start()

    def left_3():
        for k in range(1, SIDE):
            lxc(k, along(x, -k)).wait_recv()
        s.ly[y] = added(s.lx, SIDE)
        for k in range(1, SIDE):
            lyc(k, y).start()

    def left_4():
        for k in range(1, SIDE):
            lyc(k, along(y, -k)).wait_recv()
        s.left[part(core * 16, 16), :] = added(s.ly, SIDE)
        lc1(core).start()

    def left_5():
        lc1(1 - core).wait_recv()
        left = s.left[...]
        gram = lax.dot_general(
            left, left, (((1,), (1,)), ((), ())), precision=lax.Precision.HIGHEST, preferred_element_type=F32
        )
        row_g = lax.broadcasted_iota(jnp.int32, (RANK, RANK), 0)
        col_g = lax.broadcasted_iota(jnp.int32, (RANK, RANK), 1)
        row_l = lax.broadcasted_iota(jnp.int32, (RANK, SHARD), 0)
        row_1 = lax.broadcasted_iota(jnp.int32, (RANK, 1), 0)

        def step(k, carry):
            gram, left = carry
            column = jnp.sum(jnp.where(col_g == k, gram, 0.0), axis=1, keepdims=True)
            pivot = jnp.sum(jnp.where(row_1 == k, column, 0.0), axis=0, keepdims=True)
            scale = 1.0 / jnp.sqrt(pivot)
            top_g = jnp.sum(jnp.where(row_g == k, gram, 0.0), axis=0, keepdims=True) * scale
            top_l = jnp.sum(jnp.where(row_l == k, left, 0.0), axis=0, keepdims=True) * scale
            below = jnp.where(row_1 > k, column * scale, 0.0)
            gram = jnp.where(row_g == k, top_g, gram - below * top_g)
            left = jnp.where(row_l == k, top_l, left - below * top_l)
            return gram, left

        _, basis = lax.fori_loop(0, RANK, step, (gram, left))
        s.basis[...] = basis
        high, middle, low = split3(basis)
        s.b3[...] = jnp.concatenate([high, middle, low], axis=0)
        s.bt6[...] = jnp.concatenate([basis, basis, middle.astype(F32), middle.astype(F32), high.astype(F32), low.astype(F32)], axis=0).T.astype(BF16)

    p_copy = pltpu.make_async_copy(s.basis, p_hbm, s.local.at[7])

    def cols_of(chunk):
        return pl.ds(STARTS[chunk], WIDTHS[chunk])

    def start_memory():
        own_a.wait()
        for d in range(1, NODES):
            a_copy(d, node(-d)).wait_recv()
        s.at[...] = s.abuf[...].reshape(NODES * TOK, SHARD).T

    def memory_of(chunk):
        cols = cols_of(chunk)
        block = s.gbuf[:, :, cols].reshape(NODES * TOK, WIDTHS[chunk])
        s.mem[:, cols] = dot_nn(s.at[...], block) + s.errbuf[:, cols].astype(F32)

    def rcc(chunk):
        cols = cols_of(chunk)
        return remote(s.rs.at[:, cols], s.rc.at[:, cols], s.rc_s.at[chunk], s.rc_r.at[chunk], twin)

    def rxc(chunk, k, at):
        region = s.rx.at[at, :, cols_of(chunk)]
        return remote(region, region, s.rx_s.at[chunk, k], s.rx_r.at[chunk, k], x_peer(k))

    def ryc(chunk, k, at):
        region = s.ry.at[at, :, cols_of(chunk)]
        return remote(region, region, s.ry_s.at[chunk, k], s.ry_r.at[chunk, k], y_peer(k))

    def right_0(chunk):
        cols = cols_of(chunk)
        high, middle, low = split3(s.mem[:, cols])
        total = thirds(dot_nn(s.b3[...], high), RANK)
        second = dot_nn(s.b3[: 2 * RANK], middle)
        s.rs[:, cols] = total + (second[:RANK] + second[RANK:]) + dot_nn(s.b3[:RANK], low)
        rcc(chunk).start()

    def right_1(chunk):
        cols = cols_of(chunk)
        rcc(chunk).wait_recv()
        s.rx[x, :, cols] = s.rs[:, cols] + s.rc[:, cols]
        for k in range(1, SIDE):
            rxc(chunk, k, x).start()

    def right_2(chunk):
        cols = cols_of(chunk)
        for k in range(1, SIDE):
            rxc(chunk, k, along(x, -k)).wait_recv()
        s.ry[y, :, cols] = ((s.rx[0, :, cols] + s.rx[1, :, cols]) + s.rx[2, :, cols]) + s.rx[3, :, cols]
        for k in range(1, SIDE):
            ryc(chunk, k, y).start()

    def ne_copy(chunk):
        cols = cols_of(chunk)
        return pltpu.make_async_copy(s.errbuf.at[:, cols], ne_hbm.at[:, cols], s.out.at[chunk])

    def right_3(chunk):
        cols = cols_of(chunk)
        for k in range(1, SIDE):
            ryc(chunk, k, along(y, -k)).wait_recv()
        total = ((s.ry[0, :, cols] + s.ry[1, :, cols]) + s.ry[2, :, cols]) + s.ry[3, :, cols]
        right = total * (1.0 / REPS)
        s.qo[:, cols] = right
        high, middle, low = split3(right)
        approx = dot_nn(s.bt6[...], jnp.concatenate([high, middle, high, middle, low, high], axis=0))
        s.errbuf[:, cols] = (s.mem[:, cols] - approx).astype(BF16)
        ne_copy(chunk).start()

    def back(slot):
        plane = plane_of(slot)
        block = s.wbuf[slot].reshape(SHARD, D)
        s.avm[:, part(plane * SHARD, SHARD)] = dot_nt(s.gbuf[me], block).astype(BF16)

    def back_own(i):
        back(core * 4 + i)

    def back_twin(i):
        wc(i, 1 - core).wait_recv()
        back((1 - core) * 4 + i)

    ig_copy = pltpu.make_async_copy(s.avm, ig_hbm, s.local.at[3])

    def q_over_x():
        qz_wait()
        for k in range(1, SIDE):
            qx(k, x).start()

    def q_over_y():
        for k in range(1, SIDE):
            qx(k, along(x, -k)).wait_recv()
        for k in range(1, SIDE):
            qy(k, y).start()

    def q_over_cores():
        for k in range(1, SIDE):
            qy(k, along(y, -k)).wait_recv()
        qc(core).start()

    def q_done():
        qc(1 - core).wait_recv()

    def w_hop(i):
        wz_wait(i - 1)
        if i < 4:
            wz_start(i)
        else:
            w_start(0)

    def w_middle():
        w_wait(0)
        w_start(1)

    def w_cores():
        w_wait(1)
        for i in range(4):
            wc(i, core).start()

    tasks = {
        (0, 3): [q_over_x, lambda: w_hop(1), q_over_y, lambda: w_hop(2)],
        (1, 3): [lambda: w_hop(3), q_over_cores],
        (2, 2): [lambda: w_hop(4)],
        (2, 3): [q_done, left_0],
        (3, 1): [left_1],
        (3, 3): [w_middle, left_2],
        (4, 1): [left_3],
        (4, 2): [left_4],
        (4, 3): [left_5],
        (5, 2): [w_cores],
        (6, 1): [lambda: back_own(0), lambda: back_own(1)],
        (6, 2): [lambda: back_own(2), lambda: back_own(3)],
        (7, 1): [lambda: back_twin(0), lambda: back_twin(1)],
        (7, 2): [lambda: back_twin(2), lambda: back_twin(3), ig_copy.start],
    }
    stages = [memory_of, right_0, right_1, right_2, right_3]

    qz_start()
    wz_start(0)
    for d in (4, 3, 5, 2, 6, 1, 7):
        a_copy(d, me).start()
    ready = 5
    queue = []
    for t in range(CHUNKS + 4):
        for hop in range(4):
            chunk = t - hop
            if 0 <= chunk < CHUNKS:
                for way in range(2):
                    if hop:
                        g_arrived(way, chunk, hop - 1)
                    g_copy(way, chunk, hop).start()
            for task in tasks.get((t, hop), ()):
                task()
            if hop < 3 and t >= ready and queue:
                queue = [(c, n + 1) for c, n in queue if stages[n](c) is None and n < 4]
        if t == 3:
            start_memory()
        if t >= 4:
            for way in range(2):
                g_arrived(way, t - 4, 3)
            memory_of(t - 4)
            queue.append((t - 4, 1))
    while queue:
        queue = [(c, n + 1) for c, n in queue if stages[n](c) is None and n < 4]

    p_copy.start()
    q_copy = pltpu.make_async_copy(s.qo, qo_hbm, s.local.at[0])
    q_copy.start()
    qz_sent()
    only(0, lambda: wz(0).wait_send())
    for i in range(1, 4):
        wz(i).wait_send()
    for k in range(1, SIDE):
        qx(k, x).wait_send()
        qy(k, y).wait_send()
        lxc(k, x).wait_send()
        lyc(k, y).wait_send()
        for half in range(2):
            for step in range(2):
                w_step(half, step, k, w_where(half, step)).wait_send()
        for chunk in range(CHUNKS):
            rxc(chunk, k, x).wait_send()
            ryc(chunk, k, y).wait_send()
    qc(core).wait_send()
    lc0(core).wait_send()
    lc1(core).wait_send()
    for i in range(4):
        wc(i, core).wait_send()
    for d in range(1, NODES):
        a_copy(d, me).wait_send()
        lzc(d, me).wait_send()
    for chunk in range(CHUNKS):
        rcc(chunk).wait_send()
        for way in range(2):
            for hop in range(4):
                g_copy(way, chunk, hop).wait_send()
        ne_copy(chunk).wait()
    ig_copy.wait()
    p_copy.wait()
    q_copy.wait()


def shards(attn_out, out_grad, weight, error, q_prev):
    anywhere = pl.BlockSpec(memory_space=pl.ANY)
    input_grad, new_error, p_out, q_out = pl.pallas_call(
        fused_kernel,
        out_shape=(
            jax.ShapeDtypeStruct((TOK, FEATS), BF16),
            jax.ShapeDtypeStruct((SHARD, D), BF16),
            jax.ShapeDtypeStruct((RANK, SHARD), F32),
            jax.ShapeDtypeStruct((RANK, D), F32),
        ),
        in_specs=[anywhere] * 5,
        out_specs=[anywhere] * 4,
        scratch_shapes=list(SCRATCH.values()),
        compiler_params=pltpu.CompilerParams(
            collective_id=0, has_side_effects=True, vmem_limit_bytes=63 * 2**20
        ),
        name="powersgd",
    )(attn_out[0], out_grad[0], weight, error[0], q_prev[0])
    return input_grad[None], new_error[None], p_out, q_out[None]


def solution(mesh):
    in_specs = (
        P("rep", "node", None),
        P("rep", "node", None),
        P("node", None),
        P("rep", "node", None),
        P("node", None, None),
    )
    out_specs = (
        P("rep", "node", None),
        P("rep", "node", None),
        P(None, "node"),
        P("node", None, None),
    )
    return jax.shard_map(shards, mesh=mesh, in_specs=in_specs, out_specs=out_specs, check_vma=False)
```

time: 649 us -> 285 us (0.44)
  waiting for transfers between devices: 456 us -> 0 us
  Pallas kernels: 0 us -> 279 us
  blocking collectives: 123 us -> 0 us
  matrix products: 46.2 us -> 0 us
  between operations: 13.8 us -> 0.65 us
  other arithmetic: 7.51 us -> 0 us
    reduce_scatter x1 -> x0, waiting for transfers between devices: 324 us -> none  [shards(): lax.psum_scatter(lax.dot_general(feats, cotan, (((0,), (0,)), ((), ())),...]
    pallas_call x0 -> x1, Pallas kernels: none -> 279 us  [shards(): pl.pallas_call(fused_kernel, out_shape=(jax.ShapeDtypeStruct((TOK, FEATS)...]
    psum x1 -> x0, blocking collectives: 123 us -> none  [shards(): left = lax.psum(left_local, 'rep')]
    psum x1 -> x0, waiting for transfers between devices: 106 us -> none  [shards(): right = lax.psum(right_local, 'rep') / lax.axis_size('rep')]
    dot_general x6 -> x0, matrix products: 46 us -> none  [the longest x1 16.3 us: shards(): lax.dot_general(feats, cotan, (((0,), (0,)), ((), ())), preferred_element...]
    all_gather x1 -> x0, waiting for transfers between devices: 25.4 us -> none  [shards(): lax.all_gather(weight, 'node', axis=0, tiled=True)]
    another operation x5 -> x0, other arithmetic: 6.68 us -> none  [the longest x3 3.6 us: shards(): lower_factor = jnp.linalg.cholesky(gram)]
  transfers between devices with their start and end apart: 3 -> 0, of which waited for: 3 -> 0; matrix products, arithmetic and copies ran while one was open for 5% -> 0% of each run, Pallas kernels for 0% -> 0%
where the time goes in v2:
time: 285 us
  Pallas kernels  279 us (98%)
  local copies, waits for them, and re-layouts  5.37 us (2%)
    pallas_call x1, Pallas kernels, shards(): pl.pallas_call(fused_kernel, out_shape=(jax.ShapeDtypeStruct((TOK, FEATS)...  279 us

profile of v2, /device:TPU:1, one launch (start us, length us, event | category | flops | bytes accessed | tf_op | source)
XLA Modules:
  0.0 284.8 jit_solution(114459285602201224)
XLA Ops:
  0.6 278.8 %powersgd.1 = (bf16[320,2048]{1,0:T(8,128)(2,1)}, bf16[256,3968]{1,0:T(8,128)(2,1)}, f32[32,256]{1,0:T(8,128)}, f32[32,3968]{1,0:T(8,128)}) custom-call(bf16[320,2048]{1,0:T(8,128)(2,1)} %bitcast.11, bf16[320,3968]{1,0:T(8,128)(2,1)} %bitcast.7, bf16[256,3968]{1,0:T(8,128)(2,1)} %w_hbm.1, bf16[256,3968]{1,0:T(8,128)(2,1)} %bitcast.9, f32[32,3968]{1,0:T(8,128)} %bitcast.12), custom_call_target="tpu_custom_call" | custom-call | tf_op jit(solution)/shard_map/powersgd/pallas_call | solution.py:589
  279.5 0.0 copy-start
  279.5 2.7 copy.13
  282.1 0.0 copy-done
  282.1 0.0 copy-start.2
  282.1 0.0 copy-start.1
  282.1 1.3 copy.14
  283.4 0.0 copy-done.2
  283.4 0.6 copy.15
  284.1 0.0 copy-done.1
  284.1 0.8 copy.16
Async XLA Ops:
  279.5 2.7 copy-start
  282.1 1.3 copy-start.2
  282.1 1.9 copy-start.1

commit v3 on v2

--- a/solution.py
+++ b/solution.py
@@ -18,9 +18,13 @@
 FEATS = NODES * SHARD
 D = 3968
 WIDE = 4096
-WIDTHS = (640, 640, 640, 640, 512, 512, 256, 128)
+WIDTHS = (768, 768, 640, 640, 512, 384, 128, 128)
 STARTS = tuple(sum(WIDTHS[:i]) for i in range(len(WIDTHS)))
 CHUNKS = len(WIDTHS)
+FAST = 6
+FAST_AT = STARTS[FAST]
+CALM = CHUNKS - 1
+AHEAD = 1
 SPLIT = 160
 
 DMA = pltpu.SemaphoreType.DMA
@@ -46,10 +50,12 @@
     b3=pltpu.VMEM((3 * RANK, SHARD), BF16),
     bt6=pltpu.VMEM((SHARD, 6 * RANK), BF16),
     rs=pltpu.VMEM((RANK, D), F32),
-    rc=pltpu.VMEM((RANK, D), F32),
-    rx=pltpu.VMEM((SIDE, RANK, D), F32),
-    ry=pltpu.VMEM((SIDE, RANK, D), F32),
+    rc=pltpu.VMEM((RANK // 2, D), F32),
+    rx=pltpu.VMEM((SIDE, RANK // 2, D), F32),
+    ry=pltpu.VMEM((SIDE, RANK // 2, D), F32),
     qo=pltpu.VMEM((RANK, D), F32),
+    rf=pltpu.VMEM((2 * SIDE, RANK, D - FAST_AT), F32),
+    rg=pltpu.VMEM((SIDE, RANK, D - FAST_AT), F32),
     local=DMA((8,)),
     out=DMA((CHUNKS,)),
     a_s=DMA((NODES,)), a_r=DMA((NODES,)),
@@ -67,6 +73,8 @@
     lx_s=DMA((4,)), lx_r=DMA((4,)),
     ly_s=DMA((4,)), ly_r=DMA((4,)),
     rc_s=DMA((CHUNKS,)), rc_r=DMA((CHUNKS,)),
+    rd_s=DMA((CHUNKS,)), rd_r=DMA((CHUNKS,)),
+    rf_s=DMA((CHUNKS, 8)), rf_r=DMA((CHUNKS, 8)),
     rx_s=DMA((CHUNKS, 4)), rx_r=DMA((CHUNKS, 4)),
     ry_s=DMA((CHUNKS, 4)), ry_r=DMA((CHUNKS, 4)),
 )
@@ -118,6 +126,10 @@
     def y_peer(k):
         return {"rep": x * 2 * SIDE + along(y, k) * 2 + core}
 
+    def pair_peer(k):
+        other = lax.rem(x * 2 + core + k, 2 * SIDE)
+        return {"rep": lax.div(other, 2) * 2 * SIDE + y * 2 + lax.rem(other, 2)}
+
     twin = {"rep": x * 2 * SIDE + y * 2 + (1 - core)}
 
     def remote(src, dst, send_sem, recv_sem, device):
@@ -127,7 +139,7 @@
         )
 
     def plane_of(slot):
-        return lax.rem(me + jnp.where(slot < 4, 7 - slot, slot - 4), NODES)
+        return lax.rem(me + (jnp.where(slot < 4, 7 - slot, slot - 4)), NODES)
 
     def part(start, size):
         return pl.ds(pl.multiple_of(start, size), size)
@@ -137,7 +149,7 @@
 
     barrier = pltpu.get_barrier_semaphore()
     friends = [z_peer(d) for d in range(1, NODES)]
-    friends += [x_peer(k) for k in range(1, SIDE)] + [y_peer(k) for k in range(1, SIDE)] + [twin]
+    friends += [pair_peer(k) for k in range(1, 2 * SIDE)] + [y_peer(k) for k in range(1, SIDE)]
     for friend in friends:
         pl.semaphore_signal(barrier, inc=1, device_id=friend, device_id_type=MESH)
 
@@ -279,26 +291,26 @@
             region, region, s.g_s.at[way, chunk, hop], s.g_r.at[way, chunk, hop], z_peer(1 if way == 0 else -1)
         ).wait_recv()
 
-    def left_terms():
+    def inputs_here():
         own_g.wait()
         all_a.wait()
         own_e.wait()
 
-        def pair(half, carry):
-            for i in range(2):
-                pieces = split3(s.qbuf[2 * half + i, :, pl.ds(0, D)])
-                for j in range(3):
-                    s.qsp[pl.ds(64 * j + 32 * i, RANK), :] = pieces[j]
-            pieces = split3(thirds(dot_nt(s.qsp[...], s.gbuf[me]), 2 * RANK))
-            for i in range(2):
-                plane = plane_of(2 * half + i)
-                stacked = jnp.concatenate([piece[RANK * i : RANK * (i + 1)] for piece in pieces], axis=0)
-                s.lbuf[plane] = thirds(dot_nn(stacked, s.avm[:, part(plane * SHARD, SHARD)]), RANK)
-            return carry
-
-        lax.fori_loop(0, 4, pair, 0)
+    def left_pair(half):
+        for i in range(2):
+            pieces = split3(s.qbuf[2 * half + i, :, pl.ds(0, D)])
+            for j in range(3):
+                s.qsp[pl.ds(64 * j + 32 * i, RANK), :] = pieces[j]
+        pieces = split3(thirds(dot_nt(s.qsp[...], s.gbuf[me]), 2 * RANK))
+        for i in range(2):
+            plane = plane_of(2 * half + i)
+            stacked = jnp.concatenate([piece[RANK * i : RANK * (i + 1)] for piece in pieces], axis=0)
+            s.lbuf[plane] = thirds(dot_nn(stacked, s.avm[:, part(plane * SHARD, SHARD)]), RANK)
+
+    def left_own():
         pieces = split3(s.qloc[:, pl.ds(0, D)])
         s.lbuf[me] += thirds(dot_nt(jnp.concatenate(pieces, axis=0), s.errbuf[...]), RANK)
+        lc0(core).start()
 
     def lc0(at):
         return remote(
@@ -318,10 +330,6 @@
     def lc1(at):
         region = s.left.at[part(at * 16, 16)]
         return remote(region, region, s.lc_s.at[1], s.lc_r.at[1], twin)
-
-    def left_0():
-        left_terms()
-        lc0(core).start()
 
     def left_1():
         lc0(core).wait_recv()
@@ -403,7 +411,12 @@
 
     def rcc(chunk):
         cols = cols_of(chunk)
-        return remote(s.rs.at[:, cols], s.rc.at[:, cols], s.rc_s.at[chunk], s.rc_r.at[chunk], twin)
+        other = part((1 - core) * 16, 16)
+        return remote(s.rs.at[other, cols], s.rc.at[:, cols], s.rc_s.at[chunk], s.rc_r.at[chunk], twin)
+
+    def rdc(chunk, at):
+        region = s.qo.at[part(at * 16, 16), cols_of(chunk)]
+        return remote(region, region, s.rd_s.at[chunk], s.rd_r.at[chunk], twin)
 
     def rxc(chunk, k, at):
         region = s.rx.at[at, :, cols_of(chunk)]
@@ -413,18 +426,21 @@
         region = s.ry.at[at, :, cols_of(chunk)]
         return remote(region, region, s.ry_s.at[chunk, k], s.ry_r.at[chunk, k], y_peer(k))
 
-    def right_0(chunk):
+    def right_local(chunk):
         cols = cols_of(chunk)
         high, middle, low = split3(s.mem[:, cols])
         total = thirds(dot_nn(s.b3[...], high), RANK)
         second = dot_nn(s.b3[: 2 * RANK], middle)
-        s.rs[:, cols] = total + (second[:RANK] + second[RANK:]) + dot_nn(s.b3[:RANK], low)
+        return total + (second[:RANK] + second[RANK:]) + dot_nn(s.b3[:RANK], low)
+
+    def right_0(chunk):
+        s.rs[:, cols_of(chunk)] = right_local(chunk)
         rcc(chunk).start()
 
     def right_1(chunk):
         cols = cols_of(chunk)
         rcc(chunk).wait_recv()
-        s.rx[x, :, cols] = s.rs[:, cols] + s.rc[:, cols]
+        s.rx[x, :, cols] = s.rs[part(core * 16, 16), cols] + s.rc[:, cols]
         for k in range(1, SIDE):
             rxc(chunk, k, x).start()
 
@@ -445,12 +461,58 @@
         for k in range(1, SIDE):
             ryc(chunk, k, along(y, -k)).wait_recv()
         total = ((s.ry[0, :, cols] + s.ry[1, :, cols]) + s.ry[2, :, cols]) + s.ry[3, :, cols]
-        right = total * (1.0 / REPS)
-        s.qo[:, cols] = right
+        s.qo[part(core * 16, 16), cols] = total * (1.0 / REPS)
+        rdc(chunk, core).start()
+
+    def right_4(chunk):
+        cols = cols_of(chunk)
+        rdc(chunk, 1 - core).wait_recv()
+        finish(chunk, s.qo[:, cols])
+
+    def finish(chunk, right):
+        cols = cols_of(chunk)
         high, middle, low = split3(right)
         approx = dot_nn(s.bt6[...], jnp.concatenate([high, middle, high, middle, low, high], axis=0))
         s.errbuf[:, cols] = (s.mem[:, cols] - approx).astype(BF16)
         ne_copy(chunk).start()
+
+    def short(chunk):
+        return pl.ds(STARTS[chunk] - FAST_AT, WIDTHS[chunk])
+
+    place = x * 2 + core
+
+    def rfc(chunk, k, at):
+        region = s.rf.at[at, :, short(chunk)]
+        return remote(region, region, s.rf_s.at[chunk, k], s.rf_r.at[chunk, k], pair_peer(k))
+
+    def rgc(chunk, k, at):
+        region = s.rg.at[at, :, short(chunk)]
+        return remote(region, region, s.ry_s.at[chunk, k], s.ry_r.at[chunk, k], y_peer(k))
+
+    def fast_0(chunk):
+        s.rf[place, :, short(chunk)] = right_local(chunk)
+        for k in range(1, 2 * SIDE):
+            rfc(chunk, k, place).start()
+
+    def fast_1(chunk):
+        for k in range(1, 2 * SIDE):
+            rfc(chunk, k, lax.rem(place + 2 * SIDE - k, 2 * SIDE)).wait_recv()
+        total = s.rf[0, :, short(chunk)]
+        for i in range(1, 2 * SIDE):
+            total = total + s.rf[i, :, short(chunk)]
+        s.rg[y, :, short(chunk)] = total
+        for k in range(1, SIDE):
+            rgc(chunk, k, y).start()
+
+    def fast_2(chunk):
+        for k in range(1, SIDE):
+            rgc(chunk, k, along(y, -k)).wait_recv()
+        total = s.rg[0, :, short(chunk)]
+        for i in range(1, SIDE):
+            total = total + s.rg[i, :, short(chunk)]
+        right = total * (1.0 / REPS)
+        s.qo[:, cols_of(chunk)] = right
+        finish(chunk, right)
 
     def back(slot):
         plane = plane_of(slot)
@@ -504,80 +566,150 @@
     tasks = {
         (0, 3): [q_over_x, lambda: w_hop(1), q_over_y, lambda: w_hop(2)],
         (1, 3): [lambda: w_hop(3), q_over_cores],
-        (2, 2): [lambda: w_hop(4)],
-        (2, 3): [q_done, left_0],
-        (3, 1): [left_1],
-        (3, 3): [w_middle, left_2],
-        (4, 1): [left_3],
-        (4, 2): [left_4],
-        (4, 3): [left_5],
-        (5, 2): [w_cores],
-        (6, 1): [lambda: back_own(0), lambda: back_own(1)],
-        (6, 2): [lambda: back_own(2), lambda: back_own(3)],
-        (7, 1): [lambda: back_twin(0), lambda: back_twin(1)],
-        (7, 2): [lambda: back_twin(2), lambda: back_twin(3), ig_copy.start],
+        (2, 1): [inputs_here],
+        (2, 2): [lambda: w_hop(4), q_done, lambda: left_pair(0)],
+        (2, 3): [lambda: left_pair(1)],
+        (3, 0): [lambda: left_pair(2)],
+        (3, 1): [lambda: left_pair(3)],
+        (3, 2): [left_own],
+        (3, 3): [left_1, w_middle],
+        (4, 2): [left_2],
+        (4, 3): [left_3],
+        (5, 0): [left_4],
+        (5, 1): [left_5],
+        (5, 2): [w_cores, p_copy.start],
+        (6, 1): [lambda: back_own(0)],
+        (6, 2): [lambda: back_own(1)],
+        (6, 3): [lambda: back_own(2), lambda: early_sent(), lambda: left_sent()],
+        (7, 0): [lambda: back_own(3)],
+        (7, 1): [lambda: back_twin(0)],
+        (7, 2): [lambda: back_twin(1)],
+        (7, 3): [lambda: back_twin(2), lambda: w_sent()],
+        (8, 1): [lambda: back_twin(3), ig_copy.start],
     }
-    stages = [memory_of, right_0, right_1, right_2, right_3]
+    slow = [memory_of, right_0, right_1, right_2, right_3, right_4]
+    fast = [memory_of, fast_0, fast_1, fast_2]
+
+    def stages_of(chunk):
+        return slow if chunk < FAST else fast
+
+    q_copy = pltpu.make_async_copy(s.qo, qo_hbm, s.local.at[0])
+    queue, unsent = [], []
+
+    def early_sent():
+        only(0, lambda: qz(0).wait_send())
+        only(0, lambda: wz(0).wait_send())
+        for i in range(1, 4):
+            qz(i).wait_send()
+            wz(i).wait_send()
+        for d in range(1, NODES):
+            a_copy(d, me).wait_send()
+        for k in range(1, SIDE):
+            qx(k, x).wait_send()
+            qy(k, y).wait_send()
+        qc(core).wait_send()
+
+    def left_sent():
+        lc0(core).wait_send()
+        lc1(core).wait_send()
+        for d in range(1, NODES):
+            lzc(d, me).wait_send()
+        for k in range(1, SIDE):
+            lxc(k, x).wait_send()
+            lyc(k, y).wait_send()
+
+    def w_sent():
+        for half in range(2):
+            for step in range(2):
+                for k in range(1, SIDE):
+                    w_step(half, step, k, w_where(half, step)).wait_send()
+        for i in range(4):
+            wc(i, core).wait_send()
+
+    def g_sent(t):
+        for hop in range(4):
+            if 0 <= t - hop < CHUNKS:
+                for way in range(2):
+                    g_copy(way, t - hop, hop).wait_send()
+
+    def right_sent(chunk, stage):
+        if chunk < FAST:
+            if stage == 1:
+                rcc(chunk).wait_send()
+            if stage == 4:
+                rdc(chunk, core).wait_send()
+            for k in range(1, SIDE):
+                if stage == 2:
+                    rxc(chunk, k, x).wait_send()
+                if stage == 3:
+                    ryc(chunk, k, y).wait_send()
+        else:
+            for k in range(1, 2 * SIDE):
+                if stage == 1:
+                    rfc(chunk, k, place).wait_send()
+                if stage == 2 and k < SIDE:
+                    rgc(chunk, k, y).wait_send()
+
+    def advance():
+        moved = []
+        for chunk, stage in queue:
+            stages_of(chunk)[stage](chunk)
+            unsent.append((chunk, stage))
+            if stage + 1 < len(stages_of(chunk)):
+                moved.append((chunk, stage + 1))
+        queue[:] = moved
+
+    def own(chunk):
+        if chunk < CHUNKS:
+            for way in range(2):
+                g_copy(way, chunk, 0).start()
 
     qz_start()
     wz_start(0)
     for d in (4, 3, 5, 2, 6, 1, 7):
         a_copy(d, me).start()
-    ready = 5
-    queue = []
+    for chunk in range(AHEAD):
+        own(chunk)
     for t in range(CHUNKS + 4):
+        own(t + AHEAD)
         for hop in range(4):
             chunk = t - hop
-            if 0 <= chunk < CHUNKS:
+            if hop and 0 <= chunk < CHUNKS:
                 for way in range(2):
-                    if hop:
-                        g_arrived(way, chunk, hop - 1)
+                    g_arrived(way, chunk, hop - 1)
                     g_copy(way, chunk, hop).start()
             for task in tasks.get((t, hop), ()):
                 task()
-            if hop < 3 and t >= ready and queue:
-                queue = [(c, n + 1) for c, n in queue if stages[n](c) is None and n < 4]
+            if 5 <= t < CALM and hop in (2, 3):
+                advance()
+        if 4 <= t < CHUNKS:
+            g_sent(t - 4)
+            for chunk, stage in unsent[:-8]:
+                right_sent(chunk, stage)
+            del unsent[:-8]
         if t == 3:
             start_memory()
+        if t >= CALM:
+            advance()
         if t >= 4:
             for way in range(2):
                 g_arrived(way, t - 4, 3)
             memory_of(t - 4)
-            queue.append((t - 4, 1))
+            if t >= CALM:
+                stages_of(t - 4)[1](t - 4)
+                unsent.append((t - 4, 1))
+            queue.append((t - 4, 2 if t >= CALM else 1))
+    for t in range(CHUNKS - 4, CHUNKS):
+        g_sent(t)
     while queue:
-        queue = [(c, n + 1) for c, n in queue if stages[n](c) is None and n < 4]
-
-    p_copy.start()
-    q_copy = pltpu.make_async_copy(s.qo, qo_hbm, s.local.at[0])
+        advance()
+
     q_copy.start()
-    qz_sent()
-    only(0, lambda: wz(0).wait_send())
-    for i in range(1, 4):
-        wz(i).wait_send()
-    for k in range(1, SIDE):
-        qx(k, x).wait_send()
-        qy(k, y).wait_send()
-        lxc(k, x).wait_send()
-        lyc(k, y).wait_send()
-        for half in range(2):
-            for step in range(2):
-                w_step(half, step, k, w_where(half, step)).wait_send()
-        for chunk in range(CHUNKS):
-            rxc(chunk, k, x).wait_send()
-            ryc(chunk, k, y).wait_send()
-    qc(core).wait_send()
-    lc0(core).wait_send()
-    lc1(core).wait_send()
-    for i in range(4):
-        wc(i, core).wait_send()
-    for d in range(1, NODES):
-        a_copy(d, me).wait_send()
-        lzc(d, me).wait_send()
+    for chunk, stage in unsent:
+        right_sent(chunk, stage)
+    for t in range(CHUNKS, CHUNKS + 4):
+        g_sent(t)
     for chunk in range(CHUNKS):
-        rcc(chunk).wait_send()
-        for way in range(2):
-            for hop in range(4):
-                g_copy(way, chunk, hop).wait_send()
         ne_copy(chunk).wait()
     ig_copy.wait()
     p_copy.wait()

time: 285 us -> 269 us (0.944)
  Pallas kernels: 279 us -> 263 us
    pallas_call x1, Pallas kernels: 279 us -> 263 us  [shards(): pl.pallas_call(fused_kernel, out_shape=(jax.ShapeDtypeStruct((TOK, FEATS)...]
where the time goes in v3:
time: 269 us
  Pallas kernels  263 us (98%)
  local copies, waits for them, and re-layouts  5.37 us (2%)
    pallas_call x1, Pallas kernels, shards(): pl.pallas_call(fused_kernel, out_shape=(jax.ShapeDtypeStruct((TOK, FEATS)...  263 us

profile of v3, /device:TPU:1, one launch (start us, length us, event | category | flops | bytes accessed | tf_op | source)
XLA Modules:
  0.0 268.6 jit_solution(7936567469441664364)
XLA Ops:
  0.6 262.6 %powersgd.1 = (bf16[320,2048]{1,0:T(8,128)(2,1)}, bf16[256,3968]{1,0:T(8,128)(2,1)}, f32[32,256]{1,0:T(8,128)}, f32[32,3968]{1,0:T(8,128)}) custom-call(bf16[320,2048]{1,0:T(8,128)(2,1)} %bitcast.11, bf16[320,3968]{1,0:T(8,128)(2,1)} %bitcast.7, bf16[256,3968]{1,0:T(8,128)(2,1)} %w_hbm.1, bf16[256,3968]{1,0:T(8,128)(2,1)} %bitcast.9, f32[32,3968]{1,0:T(8,128)} %bitcast.12), custom_call_target="tpu_custom_call" | custom-call | tf_op jit(solution)/shard_map/powersgd/pallas_call | solution.py:721
  263.3 0.0 copy-start
  263.3 2.7 copy.13
  265.9 0.0 copy-done
  265.9 0.0 copy-start.2
  265.9 0.0 copy-start.1
  265.9 1.3 copy.14
  267.2 0.0 copy-done.2
  267.2 0.6 copy.15
  267.9 0.0 copy-done.1
  267.9 0.8 copy.16
Async XLA Ops:
  263.3 2.7 copy-start
  265.9 1.3 copy-start.2
  265.9 1.9 copy-start.1

commit v4 on v3

--- a/solution.py
+++ b/solution.py
@@ -584,8 +584,7 @@
         (7, 0): [lambda: back_own(3)],
         (7, 1): [lambda: back_twin(0)],
         (7, 2): [lambda: back_twin(1)],
-        (7, 3): [lambda: back_twin(2), lambda: w_sent()],
-        (8, 1): [lambda: back_twin(3), ig_copy.start],
+        (7, 3): [lambda: back_twin(2), lambda: back_twin(3), ig_copy.start, lambda: w_sent()],
     }
     slow = [memory_of, right_0, right_1, right_2, right_3, right_4]
     fast = [memory_of, fast_0, fast_1, fast_2]
@@ -651,13 +650,12 @@
                     rgc(chunk, k, y).wait_send()
 
     def advance():
-        moved = []
-        for chunk, stage in queue:
+        moved = [(chunk, stage) for chunk, stage in queue if stage + 1 < len(stages_of(chunk))]
+        last = [(chunk, stage) for chunk, stage in queue if stage + 1 == len(stages_of(chunk))]
+        for chunk, stage in moved + last:
             stages_of(chunk)[stage](chunk)
             unsent.append((chunk, stage))
-            if stage + 1 < len(stages_of(chunk)):
-                moved.append((chunk, stage + 1))
-        queue[:] = moved
+        queue[:] = [(chunk, stage + 1) for chunk, stage in moved]
 
     def own(chunk):
         if chunk < CHUNKS:
@@ -682,6 +680,12 @@
                 task()
             if 5 <= t < CALM and hop in (2, 3):
                 advance()
+            if t >= CALM and hop and queue:
+                chunk, stage = queue.pop(0)
+                stages_of(chunk)[stage](chunk)
+                unsent.append((chunk, stage))
+                if stage + 1 < len(stages_of(chunk)):
+                    queue.append((chunk, stage + 1))
         if 4 <= t < CHUNKS:
             g_sent(t - 4)
             for chunk, stage in unsent[:-8]:
@@ -689,8 +693,6 @@
             del unsent[:-8]
         if t == 3:
             start_memory()
-        if t >= CALM:
-            advance()
         if t >= 4:
             for way in range(2):
                 g_arrived(way, t - 4, 3)

time: 269 us -> 267 us (level)
  no operation moved by 1% of the time
where the time goes in v4:
time: 267 us
  Pallas kernels  261 us (98%)
  local copies, waits for them, and re-layouts  5.37 us (2%)
    pallas_call x1, Pallas kernels, shards(): pl.pallas_call(fused_kernel, out_shape=(jax.ShapeDtypeStruct((TOK, FEATS)...  261 us
    unnamed x10, local copies, waits for them, and re-layouts  5.37 us

profile of v4, /device:TPU:1, one launch (start us, length us, event | category | flops | bytes accessed | tf_op | source)
XLA Modules:
  0.0 266.6 jit_solution(8772577400357336189)
XLA Ops:
  0.6 260.5 %powersgd.1 = (bf16[320,2048]{1,0:T(8,128)(2,1)}, bf16[256,3968]{1,0:T(8,128)(2,1)}, f32[32,256]{1,0:T(8,128)}, f32[32,3968]{1,0:T(8,128)}) custom-call(bf16[320,2048]{1,0:T(8,128)(2,1)} %bitcast.11, bf16[320,3968]{1,0:T(8,128)(2,1)} %bitcast.7, bf16[256,3968]{1,0:T(8,128)(2,1)} %w_hbm.1, bf16[256,3968]{1,0:T(8,128)(2,1)} %bitcast.9, f32[32,3968]{1,0:T(8,128)} %bitcast.12), custom_call_target="tpu_custom_call" | custom-call | tf_op jit(solution)/shard_map/powersgd/pallas_call | solution.py:723
  261.2 0.0 copy-start
  261.2 2.7 copy.13
  263.9 0.0 copy-done
  263.9 0.0 copy-start.2
  263.9 0.0 copy-start.1
  263.9 1.3 copy.14
  265.2 0.0 copy-done.2
  265.2 0.6 copy.15
  265.8 0.0 copy-done.1
  265.8 0.8 copy.16
Async XLA Ops:
  261.2 2.7 %copy-start = (bf16[256,3968]{1,0:T(8,128)(2,1)S(1)}, bf16[256,3968]{1,0:T(8,128)(2,1)}, u32[]{:S(2)}) copy-start(bf16[256,3968]{1,0:T(8,128)(2,1)} %get-tuple-element.9) | copy-start | bytes 6094852
  263.9 1.3 copy-start.2
  263.9 1.9 copy-start.1
